TPU v7x, 32 devices: a whole 2x2x4 slice. The times are simulated.
32 devices in a mesh: grp: 2 (over core), exp: 16 (over z, y, x).
Axes of the slice: x: 2, y: 2, z: 4, core: 2. Of those that a mesh axis runs over, the one named last changes fastest.
Arguments:
- tokens: bfloat16 [4096, 7168], P('exp', 'grp'), may hold values from -6 to 6
- d_out: bfloat16 [4096, 7168], P('exp', 'grp'), may hold values from -6 to 6
- row_expert: int32 [4096], P('exp'), may hold values from 0 to 15, as said below
- w_gate_up: bfloat16 [16, 7168, 2, 1024], P('exp', 'grp'), may hold values from -0.0625 to 0.0625
- w_down: bfloat16 [16, 1024, 7168], P('exp', None, 'grp'), may hold values from -0.1875 to 0.1875
Outputs:
- token_grads: bfloat16 [4096, 7168], P('exp', 'grp')
- gate_up_grads: bfloat16 [16, 7168, 2, 1024], P('exp', 'grp')
- down_grads: bfloat16 [16, 1024, 7168], P('exp', None, 'grp')
Inputs may be any that keep to these rules, and one draw needn't show every extreme that they name: `row_expert`: in each block of 256 rows held by one index of exp, one expert, the same for every block, is named by exactly 64 rows; every other expert by at most 32 rows, and in every block some expert by exactly 32.
All inputs are finite; a program needn't handle non-finite values.
Results may differ from a plain program's by a relative error of at most 0.028.
Values may be sent and summed in bfloat16 or wider, within the bound.
No kernel may reach another device: no remote copies, remote signals or barrier semaphores. Data moves between devices by JAX's collectives and lax.ppermute only.
A program may use at most 192 MiB of HBM per device.

v0:
```python
import jax
import jax.numpy as jnp
from jax import lax
from jax.sharding import PartitionSpec as P


def slot_ranks(row_expert, expert_count):
    onehot = (row_expert[:, None] == jnp.arange(expert_count, dtype=jnp.int32)[None, :]).astype(
        jnp.int32
    )
    running = jnp.cumsum(onehot, axis=0) - 1
    return (jnp.sum(running * onehot, axis=1), jnp.sum(onehot, axis=0))


def place_rows(source_rows, slot_index, slot_total):
    blank_rows = jnp.zeros((slot_total, source_rows.shape[1]), source_rows.dtype)
    return blank_rows.at[slot_index].set(source_rows, mode="drop")


def partial_products(rows_in, grads_in, local_gate_up, local_down):
    gate_up = jnp.dot(rows_in, local_gate_up, preferred_element_type=jnp.float32)
    hidden_grads = lax.dot_general(
        grads_in, local_down, (((1,), (1,)), ((), ())), preferred_element_type=jnp.float32
    )
    return (gate_up, hidden_grads)


def activate(gate_up, hidden_grads):
    hidden_width = hidden_grads.shape[1]
    gate_value = gate_up[:, :hidden_width]
    upward = gate_up[:, hidden_width:]
    sigmoid_value = jax.nn.sigmoid(gate_value)
    activated = gate_value * sigmoid_value
    gate_slope = sigmoid_value * (1.0 + gate_value * (1.0 - sigmoid_value))
    hidden = (activated * upward).astype(jnp.bfloat16)
    branch = jnp.concatenate(
        [hidden_grads * upward * gate_slope, hidden_grads * activated], axis=1
    ).astype(jnp.bfloat16)
    return (hidden, branch)


def outer_terms(rows_in, grads_in, hidden, branch, local_gate_up):
    down_part = lax.dot_general(
        hidden, grads_in, (((0,), (0,)), ((), ())), preferred_element_type=jnp.float32
    )
    gate_up_part = lax.dot_general(
        rows_in, branch, (((0,), (0,)), ((), ())), preferred_element_type=jnp.float32
    )
    row_grads = lax.dot_general(
        branch, local_gate_up, (((1,), (1,)), ((), ())), preferred_element_type=jnp.float32
    ).astype(jnp.bfloat16)
    return (gate_up_part, down_part, row_grads)


def finish_rows(rows_in, grads_in, gate_up, hidden_grads, local_gate_up):
    hidden, branch = activate(gate_up, hidden_grads)
    return outer_terms(rows_in, grads_in, hidden, branch, local_gate_up)


def local(tokens, d_out, row_expert, w_gate_up, w_down):
    row_count, feature_share = tokens.shape
    hidden_width = w_down.shape[1]
    expert_count = lax.axis_size("exp")
    local_gate_up = w_gate_up.reshape(feature_share, 2 * hidden_width)
    local_down = w_down.reshape(hidden_width, feature_share)
    slot_rank, expert_loads = slot_ranks(row_expert, expert_count)
    hot_cap = 4 * row_count // expert_count
    slot_index = row_expert * hot_cap + slot_rank
    slot_total = expert_count * hot_cap
    sent_rows, sent_grads = (
        lax.all_to_all(
            place_rows(tokens, slot_index, slot_total).reshape(
                expert_count, hot_cap, feature_share
            ),
            "exp",
            split_axis=0,
            concat_axis=0,
            tiled=True,
        ),
        lax.all_to_all(
            place_rows(d_out, slot_index, slot_total).reshape(expert_count, hot_cap, feature_share),
            "exp",
            split_axis=0,
            concat_axis=0,
            tiled=True,
        ),
    )
    rows_in = sent_rows.reshape(slot_total, feature_share)
    grads_in = sent_grads.reshape(slot_total, feature_share)
    gate_part, hidden_part = partial_products(rows_in, grads_in, local_gate_up, local_down)
    gate_up, hidden_grads = (
        lax.psum(gate_part.astype(jnp.bfloat16), "grp").astype(jnp.float32),
        lax.psum(hidden_part.astype(jnp.bfloat16), "grp").astype(jnp.float32),
    )
    gate_up_part, down_part, row_grads = finish_rows(
        rows_in, grads_in, gate_up, hidden_grads, local_gate_up
    )
    returned = lax.all_to_all(
        row_grads.reshape(expert_count, hot_cap, feature_share),
        "exp",
        split_axis=0,
        concat_axis=0,
        tiled=True,
    )
    token_grads = returned.reshape(slot_total, feature_share)[slot_index]
    gate_up_grads = gate_up_part.astype(jnp.bfloat16).reshape(1, feature_share, 2, hidden_width)
    down_grads = down_part.astype(jnp.bfloat16).reshape(1, hidden_width, feature_share)
    return (token_grads, gate_up_grads, down_grads)


def solution(mesh):
    return jax.shard_map(
        local,
        mesh=mesh,
        in_specs=(
            P("exp", "grp"),
            P("exp", "grp"),
            P("exp"),
            P("exp", "grp", None, None),
            P("exp", None, "grp"),
        ),
        out_specs=(P("exp", "grp"), P("exp", "grp", None, None), P("exp", None, "grp")),
        check_vma=False,
    )
```

profile of v0, /device:TPU:28, one launch (start us, length us, event | category | flops | bytes accessed | tf_op | source)
XLA Modules:
  0.0 632.3 jit_solution(16722757638303725101)
XLA Ops:
  7.2 0.7 fusion.17
  7.8 0.6 reduce-window.6
  8.4 0.2 slice_reduce_fusion
  8.6 0.8 fusion.16
  9.4 0.7 compare_select_fusion
  10.1 8.5 %scatter_custom_fusion = bf16[1024,3584]{1,0:T(8,128)(2,1)} fusion(s32[256]{0:T(256)S(1)} %compare_select_fusion, bf16[256,3584]{1,0:T(8,128)(2,1)} %param.6, bf16[]{:T(256)} %constant.6.clone.1), kind=kCustom, calls=%fused_computation.21 | custom fusion | bytes 7340544 | tf_op jit(solution)/shard_map/scatter | solution.py:17
  18.6 6.9 %all-to-all-start = ((bf16[16,64,3584]{2,1,0:T(8,128)(2,1)}), bf16[16,64,3584]{2,1,0:T(8,128)(2,1)}, u32[]{:S(2)}, u32[]{:S(2)}) async-start(bf16[16,64,3584]{2,1,0:T(8,128)(2,1)} %bitcast.42), calls=%async_computation | async-start | bytes 14680064 | tf_op jit(solution)/shard_map/all_to_all | solution.py:80
  25.5 8.5 %scatter_custom_fusion.1 = bf16[1024,3584]{1,0:T(8,128)(2,1)} fusion(s32[256]{0:T(256)S(1)} %compare_select_fusion, bf16[256,3584]{1,0:T(8,128)(2,1)} %param.5, bf16[]{:T(256)} %constant.6.clone.1), kind=kCustom, calls=%fused_computation.19 | custom fusion | bytes 7340544 | tf_op jit(solution)/shard_map/scatter | solution.py:17
  34.1 157.7 %all-to-all-done = bf16[16,64,3584]{2,1,0:T(8,128)(2,1)} async-done(((bf16[16,64,3584]{2,1,0:T(8,128)(2,1)}), bf16[16,64,3584]{2,1,0:T(8,128)(2,1)}, u32[]{:S(2)}, u32[]{:S(2)}) %all-to-all-start) | async-done | bytes 7340064 | tf_op jit(solution)/shard_map/all_to_all | solution.py:80
  191.8 6.0 all-to-all-start.1
  197.8 0.0 all-reduce.3.cloned.1.call-start
  197.9 16.0 %copy.12 = bf16[448,8,2,1024]{3,1,2,0:T(8,128)(2,1)} copy(bf16[448,8,2,1024]{3,2,1,0:T(2,128)(2,1)} %bitcast.43) | data formatting | bytes 29360128
  213.9 13.2 %fusion.11 = bf16[1024,1024]{1,0:T(8,128)(2,1)} fusion(bf16[1024,3584]{1,0:T(8,128)(2,1)} %bitcast.3, bf16[1,1024,3584]{2,1,0:T(8,128)(2,1)} %param.9), kind=kOutput, calls=%fused_computation.23 | convolution fusion | flops 7517241344 | bytes 16777216 | tf_op jit(solution)/shard_map/dot_general | solution.py:22
  227.1 132.4 %all-to-all-done.1 = bf16[16,64,3584]{2,1,0:T(8,128)(2,1)} async-done(((bf16[16,64,3584]{2,1,0:T(8,128)(2,1)}), bf16[16,64,3584]{2,1,0:T(8,128)(2,1)}, u32[]{:S(2)}, u32[]{:S(2)}) %all-to-all-start.1) | async-done | bytes 7340064 | tf_op jit(solution)/shard_map/all_to_all | solution.py:71
  359.6 21.0 %convolution_convert_fusion.3 = bf16[1024,2048]{1,0:T(8,128)(2,1)} fusion(bf16[1024,3584]{1,0:T(8,128)(2,1)} %bitcast.6, bf16[3584,2048]{1,0:T(8,128)(2,1)} %bitcast.44), kind=kOutput, calls=%fused_computation.18 | convolution fusion | flops 15034482688 | bytes 26214400 | tf_op jit(solution)/shard_map/dot_general | solution.py:21
  380.6 0.0 all-reduce.3.cloned.1.call-update
  380.6 32.5 %all-reduce.3.cloned.1.call-done = (bf16[1024,1024]{1,0:T(8,128)(2,1)}, bf16[1024,2048]{1,0:T(8,128)(2,1)}) async-done(((bf16[1024,1024]{1,0:T(8,128)(2,1)}, bf16[1024,2048]{1,0:T(8,128)(2,1)}), (bf16[1024,1024]{1,0:T(8,128)(2,1)}, bf16[1024,2048]{1,0:T(8,128)(2,1)})) %all-reduce.3.cloned.1.call-update) | async-done | bytes 6291472 | tf_op jit(solution)/shard_map/psum | solution.py:93
  413.1 0.0 copy-start.1
  413.1 3.4 convert_element_type.34
  416.5 0.0 copy-start
  416.6 0.0 copy-done.1
  416.6 4.0 fusion.4
  420.6 0.0 copy-done
  420.6 21.3 %convolution_convert_fusion.2 = bf16[1024,3584]{1,0:T(8,128)(2,1)} fusion(bf16[3584,2048]{1,0:T(8,128)(2,1)} %bitcast.45, bf16[1024,1024]{1,0:T(8,128)(2,1)} %get-tuple-element.12, bf16[1024,1024]{1,0:T(8,128)(2,1)S(1)} %get-tuple-element.11), kind=kOutput, calls=%fused_computation.5 | convolution fusion | flops 15044444160 | bytes 26214400 | tf_op jit(solution)/shard_map/dot_general | solution.py:49
  441.9 7.3 %all-to-all-start.2 = ((bf16[16,64,3584]{2,1,0:T(8,128)(2,1)}), bf16[16,64,3584]{2,1,0:T(8,128)(2,1)}, u32[]{:S(2)}, u32[]{:S(2)}) async-start(bf16[16,64,3584]{2,1,0:T(8,128)(2,1)} %bitcast.47), calls=%async_computation.2 | async-start | bytes 14680064 | tf_op jit(solution)/shard_map/all_to_all | solution.py:98
  449.2 21.9 %convolution_convert_fusion = bf16[3584,2048]{0,1:T(8,128)(2,1)} fusion(bf16[1024,3584]{1,0:T(8,128)(2,1)} %bitcast.6, bf16[1024,1024]{1,0:T(8,128)(2,1)} %get-tuple-element.12, bf16[1024,1024]{1,0:T(8,128)(2,1)S(1)} %get-tuple-element.11), kind=kOutput, calls=%fused_computation.3 | convolution fusion | flops 15048114176 | bytes 26214400 | tf_op jit(solution)/shard_map/dot_general | solution.py:46
  471.1 36.5 %copy.10 = bf16[1,3584,2,1024]{3,2,1,0:T(2,128)(2,1)} copy(bf16[1,3584,2,1024]{1,3,2,0:T(8,128)(2,1)} %bitcast.46) | data formatting | bytes 29360128
  507.6 15.1 %fusion.2 = bf16[1,1024,3584]{2,1,0:T(8,128)(2,1)} fusion(bf16[1024,3584]{1,0:T(8,128)(2,1)} %bitcast.3, f32[1024,2048]{1,0:T(8,128)} %copy-done), kind=kOutput, calls=%fused_computation.8 | convolution fusion | flops 7526154240 | bytes 23068672 | tf_op jit(solution)/shard_map/dot_general | solution.py:43
  522.7 93.5 %all-to-all-done.2 = bf16[16,64,3584]{2,1,0:T(8,128)(2,1)} async-done(((bf16[16,64,3584]{2,1,0:T(8,128)(2,1)}), bf16[16,64,3584]{2,1,0:T(8,128)(2,1)}, u32[]{:S(2)}, u32[]{:S(2)}) %all-to-all-start.2) | async-done | bytes 7340064 | tf_op jit(solution)/shard_map/all_to_all | solution.py:98
  616.2 8.8 %gather_fusion = bf16[256,3584]{1,0:T(8,128)(2,1)} fusion(bf16[1024,3584]{1,0:T(8,128)(2,1)} %bitcast.8, s32[1024]{0:T(1024)S(1)} %pad_clamp_fusion), kind=kCustom, calls=%fused_computation | custom fusion | bytes 3671040 | tf_op jit(solution)/shard_map/gather | solution.py:105
  (3 shorter events, 0.0 us)
Async XLA Ops:
  18.6 173.2 %all-to-all-start = ((bf16[16,64,3584]{2,1,0:T(8,128)(2,1)}), bf16[16,64,3584]{2,1,0:T(8,128)(2,1)}, u32[]{:S(2)}, u32[]{:S(2)}) async-start(bf16[16,64,3584]{2,1,0:T(8,128)(2,1)} %bitcast.42), calls=%async_computation | async-start | bytes 14680064 | tf_op jit(solution)/shard_map/all_to_all | solution.py:80
  191.8 167.8 %all-to-all-start.1 = ((bf16[16,64,3584]{2,1,0:T(8,128)(2,1)}), bf16[16,64,3584]{2,1,0:T(8,128)(2,1)}, u32[]{:S(2)}, u32[]{:S(2)}) async-start(bf16[16,64,3584]{2,1,0:T(8,128)(2,1)} %bitcast.41), calls=%async_computation.1 | async-start | bytes 14680064 | tf_op jit(solution)/shard_map/all_to_all | solution.py:71
  197.8 215.3 %all-reduce.3.cloned.1.call-start = ((), (), s32[]{:S(2)}) async-start(), calls=%async_computation.3 | async-start | bytes 12582912 | tf_op jit(solution)/shard_map/psum | solution.py:93
  413.1 3.4 copy-start.1
  416.5 4.1 copy-start
  441.9 174.3 %all-to-all-start.2 = ((bf16[16,64,3584]{2,1,0:T(8,128)(2,1)}), bf16[16,64,3584]{2,1,0:T(8,128)(2,1)}, u32[]{:S(2)}, u32[]{:S(2)}) async-start(bf16[16,64,3584]{2,1,0:T(8,128)(2,1)} %bitcast.47), calls=%async_computation.2 | async-start | bytes 14680064 | tf_op jit(solution)/shard_map/all_to_all | solution.py:98
Sparse Core Ops, SparseCore 0:
  380.7 32.3 all-reduce.2
where the time goes:
time: 642 us; the launch traced here: 632 us
  waiting for transfers between devices  416 us (65%)
  matrix products  92.5 us (14%)
  local copies, waits for them, and re-layouts  78.5 us (12%)
  starting transfers between devices  20.3 us (3%)
  between operations  14.6 us (2%)
  other arithmetic  10.2 us (2%)
    all_to_all x1, waiting for transfers between devices, local(): lax.all_to_all(place_rows(d_out, slot_index, slot_total).reshape(expert_c...  158 us
    all_to_all x1, waiting for transfers between devices, local(): lax.all_to_all(place_rows(tokens, slot_index, slot_total).reshape(expert_...  132 us
    all_to_all x1, waiting for transfers between devices, local(): lax.all_to_all(row_grads.reshape(expert_count, hot_cap, feature_share), '...  93.5 us
    unnamed x6, local copies, waits for them, and re-layouts  52.5 us
    psum x1, waiting for transfers between devices, local(): lax.psum(hidden_part.astype(jnp.bfloat16), 'grp').astype(jnp.float32)  32.5 us
    dot_general x1, matrix products, outer_terms(): lax.dot_general(rows_in, branch, (((0,), (0,)), ((), ())), preferred_elem...  21.9 us
    dot_general x1, matrix products, outer_terms(): lax.dot_general(branch, local_gate_up, (((1,), (1,)), ((), ())), preferre...  21.3 us
    dot_general x1, matrix products, partial_products(): jnp.dot(rows_in, local_gate_up, preferred_element_type=jnp.float32)  21 us
  transfers between devices with their start and end apart: 4, of which 4 were waited for; matrix products, arithmetic and copies ran while one was open for 18% of the time, Pallas kernels for 0%

commit v1 on v0

v1 whole, which is shorter than its diff:
```python
import jax
import jax.numpy as jnp
from jax import lax
from jax.sharding import PartitionSpec as P


def rank_in_expert(row_expert):
    row_count = row_expert.shape[0]
    same = row_expert[:, None] == row_expert[None, :]
    earlier = jnp.arange(row_count)[None, :] < jnp.arange(row_count)[:, None]
    return jnp.sum((same & earlier).astype(jnp.int32), axis=1)


def one_hot(index, total):
    return (index[None, :] == jnp.arange(total, dtype=jnp.int32)[:, None]).astype(jnp.bfloat16)


def place(one_hot_rows, rows):
    return lax.dot_general(
        one_hot_rows, rows, (((1,), (0,)), ((), ())), preferred_element_type=jnp.float32
    ).astype(jnp.bfloat16)


def exchange(rows, expert_count):
    slots, width = rows.shape
    return lax.all_to_all(
        rows.reshape(expert_count, slots // expert_count, width),
        "exp",
        split_axis=0,
        concat_axis=0,
        tiled=True,
    ).reshape(slots, width)


def sum_over_grp(part):
    part = part.astype(jnp.bfloat16)
    if lax.axis_size("grp") == 2:
        other = lax.ppermute(part, "grp", [(0, 1), (1, 0)])
        return part.astype(jnp.float32) + other.astype(jnp.float32)
    return lax.psum(part, "grp").astype(jnp.float32)


def activate(gate_up, hidden_grads):
    hidden_width = hidden_grads.shape[1]
    gate_value = gate_up[:, :hidden_width]
    upward = gate_up[:, hidden_width:]
    sigmoid_value = jax.nn.sigmoid(gate_value)
    activated = gate_value * sigmoid_value
    gate_slope = sigmoid_value * (1.0 + gate_value * (1.0 - sigmoid_value))
    hidden = (activated * upward).astype(jnp.bfloat16)
    branch = jnp.concatenate(
        [hidden_grads * upward * gate_slope, hidden_grads * activated], axis=1
    ).astype(jnp.bfloat16)
    return hidden, branch


def forward(rows_in, grads_in, gate_up_matrix, down_matrix):
    gate_up = sum_over_grp(jnp.dot(rows_in, gate_up_matrix, preferred_element_type=jnp.float32))
    hidden_grads = sum_over_grp(
        lax.dot_general(
            grads_in, down_matrix, (((1,), (1,)), ((), ())), preferred_element_type=jnp.float32
        )
    )
    return activate(gate_up, hidden_grads)


def row_gradients(branch, gate_up_matrix):
    return lax.dot_general(
        branch, gate_up_matrix, (((1,), (1,)), ((), ())), preferred_element_type=jnp.float32
    ).astype(jnp.bfloat16)


def outer(left, right):
    return lax.dot_general(
        left, right, (((0,), (0,)), ((), ())), preferred_element_type=jnp.float32
    ).astype(jnp.bfloat16)


def local(tokens, d_out, row_expert, w_gate_up, w_down):
    row_count, feature_share = tokens.shape
    hidden_width = w_down.shape[1]
    expert_count = lax.axis_size("exp")
    gate_up_matrix = w_gate_up.reshape(feature_share, 2 * hidden_width)
    down_matrix = w_down.reshape(hidden_width, feature_share)
    cap = 2 * row_count // expert_count
    half = cap // 2

    rank = rank_in_expert(row_expert)
    is_spill = rank >= cap
    busiest = jnp.max(jnp.where(is_spill, row_expert, -1))
    is_busiest = lax.axis_index("exp") == busiest
    spill_hot = one_hot(jnp.where(is_spill, rank - cap, -1), cap)
    chunk_hot = []
    for chunk in range(2):
        inside = (rank >= chunk * half) & (rank < (chunk + 1) * half)
        slot = row_expert * half + rank - chunk * half
        chunk_hot.append(one_hot(jnp.where(inside, slot, -1), expert_count * half))

    spill_rows = lax.all_gather(place(spill_hot, tokens), "exp", tiled=True)
    spill_grads = lax.all_gather(place(spill_hot, d_out), "exp", tiled=True)
    chunk_rows = []
    chunk_grads = []
    for hot in chunk_hot:
        chunk_rows.append(exchange(place(hot, tokens), expert_count))
        chunk_grads.append(exchange(place(hot, d_out), expert_count))

    hidden, branch = forward(spill_rows, spill_grads, gate_up_matrix, down_matrix)
    hidden = jnp.where(is_busiest, hidden, jnp.zeros_like(hidden))
    branch = jnp.where(is_busiest, branch, jnp.zeros_like(branch))
    spill_back = lax.psum_scatter(
        row_gradients(branch, gate_up_matrix), "exp", scatter_dimension=0, tiled=True
    )
    all_hidden = [hidden]
    all_branch = [branch]
    back = []
    for rows_in, grads_in in zip(chunk_rows, chunk_grads):
        hidden, branch = forward(rows_in, grads_in, gate_up_matrix, down_matrix)
        all_hidden.append(hidden)
        all_branch.append(branch)
        back.append(exchange(row_gradients(branch, gate_up_matrix), expert_count))

    all_rows = jnp.concatenate([spill_rows] + chunk_rows, axis=0)
    all_grads = jnp.concatenate([spill_grads] + chunk_grads, axis=0)
    hidden = jnp.concatenate(all_hidden, axis=0)
    branch = jnp.concatenate(all_branch, axis=0)
    gate_up_grads = outer(all_rows, branch).reshape(1, feature_share, 2, hidden_width)
    down_grads = outer(hidden, all_grads).reshape(1, hidden_width, feature_share)

    pick = jnp.concatenate([spill_hot] + chunk_hot, axis=0)
    returned = jnp.concatenate([spill_back] + back, axis=0)
    token_grads = lax.dot_general(
        pick, returned, (((0,), (0,)), ((), ())), preferred_element_type=jnp.float32
    ).astype(jnp.bfloat16)
    return (token_grads, gate_up_grads, down_grads)


def solution(mesh):
    return jax.shard_map(
        local,
        mesh=mesh,
        in_specs=(
            P("exp", "grp"),
            P("exp", "grp"),
            P("exp"),
            P("exp", "grp", None, None),
            P("exp", None, "grp"),
        ),
        out_specs=(P("exp", "grp"), P("exp", "grp", None, None), P("exp", None, "grp")),
        check_vma=False,
    )
```

time: 642 us -> 464 us (0.72)
  the two profiles are of different devices: /device:TPU:28 before, /device:TPU:0 now
where the time goes in v1:
time: 464 us; the launch traced here: 455 us
  waiting for transfers between devices  161 us (35%)
  matrix products  142 us (31%)
  starting transfers between devices  62.7 us (14%)
  local copies, waits for them, and re-layouts  55 us (12%)
  other arithmetic  19.9 us (4%)
  between operations  15 us (3%)
    all_to_all x6, waiting for transfers between devices, exchange(): lax.all_to_all(rows.reshape(expert_count, slots // expert_count, width),...  134 us
    all_to_all x6, starting transfers between devices, exchange(): lax.all_to_all(rows.reshape(expert_count, slots // expert_count, width),...  61.1 us
    unnamed x34, local copies, waits for them, and re-layouts  55 us
    dot_general x3, matrix products, row_gradients(): lax.dot_general(branch, gate_up_matrix, (((1,), (1,)), ((), ())), preferr...  40.3 us
    dot_general x2, matrix products, outer(): lax.dot_general(left, right, (((0,), (0,)), ((), ())), preferred_element_...  33.1 us
    dot_general x3, matrix products, forward(): jnp.dot(rows_in, gate_up_matrix, preferred_element_type=jnp.float32)  32.8 us
    dot_general x3, matrix products, forward(): lax.dot_general(grads_in, down_matrix, (((1,), (1,)), ((), ())), preferre...  17.7 us
    all_gather x1, waiting for transfers between devices, local(): spill_grads = lax.all_gather(place(spill_hot, d_out), 'exp', tiled=True)  16.9 us
  transfers between devices with their start and end apart: 15, of which 7 were waited for; matrix products, arithmetic and copies ran while one was open for 45% of the time, Pallas kernels for 0%

profile of v1, /device:TPU:0, one launch (start us, length us, event | category | flops | bytes accessed | tf_op | source)
XLA Modules:
  0.0 455.4 jit_solution(6285182354319972403)
XLA Ops:
  7.2 0.0 copy-start
  7.2 1.0 convert_reduce_fusion
  8.2 1.4 select_reduce_fusion
  9.5 3.4 convolution_convert_fusion.7
  12.9 8.4 %all-to-all-start.3 = ((bf16[16,16,3584]{2,1,0:T(8,128)(2,1)}), bf16[16,16,3584]{2,1,0:T(8,128)(2,1)}, u32[]{:S(2)}, u32[]{:S(2)}) async-start(bf16[16,16,3584]{2,1,0:T(8,128)(2,1)} %bitcast.61), calls=%async_computation.4 | async-start | bytes 3670016 | tf_op jit(solution)/shard_map/all_to_all | solution.py:26
  21.3 1.9 convolution_convert_fusion.6
  23.2 36.8 %all-to-all-done.3 = bf16[16,16,3584]{2,1,0:T(8,128)(2,1)} async-done(((bf16[16,16,3584]{2,1,0:T(8,128)(2,1)}), bf16[16,16,3584]{2,1,0:T(8,128)(2,1)}, u32[]{:S(2)}, u32[]{:S(2)}) %all-to-all-start.3) | async-done | bytes 1835040 | tf_op jit(solution)/shard_map/all_to_all | solution.py:26
  59.9 8.9 %all-to-all-start.4 = ((bf16[16,16,3584]{2,1,0:T(8,128)(2,1)}), bf16[16,16,3584]{2,1,0:T(8,128)(2,1)}, u32[]{:S(2)}, u32[]{:S(2)}) async-start(bf16[16,16,3584]{2,1,0:T(8,128)(2,1)} %bitcast.59), calls=%async_computation.5 | async-start | bytes 3670016 | tf_op jit(solution)/shard_map/all_to_all | solution.py:26
  68.8 0.0 all-gather.5.cloned.1.call-start
  68.9 1.1 convolution_convert_fusion.10
  70.0 0.0 all-gather.5.cloned.1.call-update
  70.0 3.4 convolution_convert_fusion.9
  73.4 38.4 %all-to-all-done.4 = bf16[16,16,3584]{2,1,0:T(8,128)(2,1)} async-done(((bf16[16,16,3584]{2,1,0:T(8,128)(2,1)}), bf16[16,16,3584]{2,1,0:T(8,128)(2,1)}, u32[]{:S(2)}, u32[]{:S(2)}) %all-to-all-start.4) | async-done | bytes 1835040 | tf_op jit(solution)/shard_map/all_to_all | solution.py:26
  111.8 17.1 %all-to-all-start = ((bf16[16,16,3584]{2,1,0:T(8,128)(2,1)}), bf16[16,16,3584]{2,1,0:T(8,128)(2,1)}, u32[]{:S(2)}, u32[]{:S(2)}) async-start(bf16[16,16,3584]{2,1,0:T(8,128)(2,1)} %bitcast.60), calls=%async_computation.1 | async-start | bytes 3670016 | tf_op jit(solution)/shard_map/all_to_all | solution.py:26
  128.9 1.9 convolution_convert_fusion.8
  130.8 52.7 %all-to-all-done = bf16[16,16,3584]{2,1,0:T(8,128)(2,1)} async-done(((bf16[16,16,3584]{2,1,0:T(8,128)(2,1)}), bf16[16,16,3584]{2,1,0:T(8,128)(2,1)}, u32[]{:S(2)}, u32[]{:S(2)}) %all-to-all-start) | async-done | bytes 1835040 | tf_op jit(solution)/shard_map/all_to_all | solution.py:26
  183.5 8.8 %all-to-all-start.1 = ((bf16[16,16,3584]{2,1,0:T(8,128)(2,1)}), bf16[16,16,3584]{2,1,0:T(8,128)(2,1)}, u32[]{:S(2)}, u32[]{:S(2)}) async-start(bf16[16,16,3584]{2,1,0:T(8,128)(2,1)} %bitcast.58), calls=%async_computation.2 | async-start | bytes 3670016 | tf_op jit(solution)/shard_map/all_to_all | solution.py:26
  192.3 0.3 all-gather.3.cloned.1.call-start
  192.6 1.1 convolution_convert_fusion.11
  193.6 0.0 all-gather.3.cloned.1.call-update
  193.7 16.1 %copy.10 = bf16[448,8,2,1024]{3,1,2,0:T(8,128)(2,1)} copy(bf16[448,8,2,1024]{3,2,1,0:T(2,128)(2,1)} %bitcast.50) | data formatting | bytes 29360128
  210.4 0.1 iota_compare_fusion
  210.5 0.0 slice-start
  210.5 5.9 %fusion.45 = bf16[256,1024]{1,0:T(8,128)(2,1)S(1)} fusion(bf16[256,3584]{1,0:T(8,128)(2,1)} %bitcast.8, bf16[1,1024,3584]{2,1,0:T(8,128)(2,1)} %param.9), kind=kOutput, calls=%fused_computation.63 | convolution fusion | flops 1879310336 | bytes 9699328 | tf_op jit(solution)/shard_map/dot_general | solution.py:60
  216.4 0.1 collective-permute-start.4
  216.5 0.0 slice-start.1
  216.5 9.8 %convolution_convert_fusion.13 = bf16[256,2048]{1,0:T(8,128)(2,1)S(1)} fusion(bf16[256,3584]{1,0:T(8,128)(2,1)} %bitcast.10, bf16[3584,2048]{1,0:T(8,128)(2,1)} %bitcast.51), kind=kOutput, calls=%fused_computation.45 | convolution fusion | flops 3758620672 | bytes 17563648 | tf_op jit(solution)/shard_map/dot_general | solution.py:58
  226.4 0.5 collective-permute-start.5
  226.9 3.6 fusion.42
  230.5 0.1 collective-permute-start.2
  230.6 4.4 all-to-all-done.1
  235.0 9.7 %convolution_convert_fusion.14 = bf16[256,2048]{1,0:T(8,128)(2,1)S(1)} fusion(bf16[256,3584]{1,0:T(8,128)(2,1)} %bitcast.4, bf16[3584,2048]{1,0:T(8,128)(2,1)} %bitcast.52), kind=kOutput, calls=%fused_computation.46 | convolution fusion | flops 3758620672 | bytes 17563648 | tf_op jit(solution)/shard_map/dot_general | solution.py:58
  244.8 0.0 copy-start.10
  244.8 0.1 collective-permute-start.3
  244.9 1.6 convert_add_fusion.1
  246.5 2.7 multiply_convert_fusion.6
  249.3 13.3 %convolution_convert_fusion.12 = bf16[512,2048]{1,0:T(8,128)(2,1)} fusion(bf16[512,3584]{1,0:T(8,128)(2,1)} %all-gather.5.cloned.1.call-done, bf16[3584,2048]{1,0:T(8,128)(2,1)} %bitcast.53), kind=kOutput, calls=%fused_computation.44 | convolution fusion | flops 7517241344 | bytes 20447232 | tf_op jit(solution)/shard_map/dot_general | solution.py:58
  262.5 0.4 collective-permute-start.1
  263.0 16.9 %all-gather.3.cloned.1.call-done = bf16[512,3584]{1,0:T(8,128)(2,1)} async-done(((bf16[32,3584]{1,0:T(8,128)(2,1)}), bf16[512,3584]{1,0:T(8,128)(2,1)}) %all-gather.3.cloned.1.call-update) | async-done | bytes 3670032 | tf_op jit(solution)/shard_map/all_gather | solution.py:100
  279.9 8.2 %fusion.39 = bf16[512,1024]{1,0:T(8,128)(2,1)S(1)} fusion(bf16[512,3584]{1,0:T(8,128)(2,1)} %all-gather.3.cloned.1.call-done, bf16[1,1024,3584]{2,1,0:T(8,128)(2,1)} %param.9), kind=kOutput, calls=%fused_computation.61 | convolution fusion | flops 3758620672 | bytes 12058624 | tf_op jit(solution)/shard_map/dot_general | solution.py:60
  288.1 0.1 collective-permute-start
  288.1 11.0 %convolution_convert_fusion.3 = bf16[256,3584]{1,0:T(8,128)(2,1)} fusion(bf16[3584,2048]{1,0:T(8,128)(2,1)} %bitcast.54, bf16[256,1024]{1,0:T(8,128)(2,1)} %get-tuple-element.14, bf16[256,1024]{1,0:T(8,128)(2,1)} %get-tuple-element.13), kind=kOutput, calls=%fused_computation.20 | convolution fusion | flops 3761111040 | bytes 17563648 | tf_op jit(solution)/shard_map/dot_general | solution.py:68
  299.2 4.4 all-to-all-start.5
  303.6 0.0 reduce-scatter.2.cloned.1.call-start
  303.6 3.1 convert_add_fusion
  306.8 0.0 copy-start.2
  306.8 3.2 multiply_convert_fusion.2
  310.0 0.4 maximum_select_fusion
  310.4 1.3 copy-done.4
  311.7 13.0 %convolution_convert_fusion.2 = bf16[512,3584]{1,0:T(8,128)(2,1)} fusion(bf16[512,2048]{1,0:T(8,128)(2,1)S(1)} %maximum_select_fusion, bf16[3584,2048]{1,0:T(8,128)(2,1)} %bitcast.55), kind=kOutput, calls=%fused_computation.19 | convolution fusion | flops 7518027776 | bytes 20447232 | tf_op jit(solution)/shard_map/dot_general | solution.py:68
  324.7 0.0 reduce-scatter.2.cloned.1.call-update
  324.8 1.6 convert_add_fusion.2
  326.4 1.7 multiply_convert_fusion.8
  328.1 0.8 copy-done.11
  328.9 16.2 %convolution_convert_fusion.4 = bf16[256,3584]{1,0:T(8,128)(2,1)} fusion(bf16[3584,2048]{1,0:T(8,128)(2,1)} %bitcast.56, bf16[256,1024]{1,0:T(8,128)(2,1)S(1)} %get-tuple-element.12, bf16[256,1024]{1,0:T(8,128)(2,1)S(1)} %get-tuple-element.11), kind=kOutput, calls=%fused_computation.21 | convolution fusion | flops 3761111040 | bytes 17563648 | tf_op jit(solution)/shard_map/dot_general | solution.py:68
  345.1 1.9 all-to-all-done.5
  347.1 13.5 %all-to-all-start.2 = ((bf16[16,16,3584]{2,1,0:T(8,128)(2,1)}), bf16[16,16,3584]{2,1,0:T(8,128)(2,1)}, u32[]{:S(2)}, u32[]{:S(2)}) async-start(bf16[16,16,3584]{2,1,0:T(8,128)(2,1)} %bitcast.5), calls=%async_computation.3 | async-start | bytes 3670016 | tf_op jit(solution)/shard_map/all_to_all | solution.py:26
  360.6 21.4 %convolution_convert_fusion = bf16[3584,2048]{0,1:T(8,128)(2,1)} fusion(bf16[256,3584]{1,0:T(8,128)(2,1)} %bitcast.10, bf16[256,3584]{1,0:T(8,128)(2,1)} %bitcast.4, bf16[512,3584]{1,0:T(8,128)(2,1)} %all-gather.5.cloned.1.call-done, bf16[256,1024]{1,0:T(8,128)(2,1)S(1)} %copy-done.8, bf16[256,1024]{1,0:T(8,128)(2,1)S(1)} %copy-done.7, ...), kind=kOutput, calls=%fused_computation | convolution fusion | flops 15082717184 | bytes 26214400 | tf_op jit(solution)/shard_map/dot_general | solution.py:74
  382.1 36.5 %copy.9 = bf16[1,3584,2,1024]{3,2,1,0:T(2,128)(2,1)} copy(bf16[1,3584,2,1024]{1,3,2,0:T(8,128)(2,1)} %bitcast.57) | data formatting | bytes 29360128
  418.6 3.0 fusion.48
  421.6 0.3 copy-done.13
  421.9 11.6 %fusion.16 = bf16[1,1024,3584]{2,1,0:T(8,128)(2,1)} fusion(bf16[256,3584]{1,0:T(8,128)(2,1)} %bitcast.8, bf16[256,3584]{1,0:T(8,128)(2,1)} %bitcast.2, bf16[512,3584]{1,0:T(8,128)(2,1)S(1)} %copy-done.13, bf16[256,1024]{1,0:T(8,128)(2,1)S(1)} %get-tuple-element.16, bf16[256,1024]{1,0:T(8,128)(2,1)S(1)} %get-tuple-element.15, bf16[512,1024]{1,0:T(8,128)(2,1)S(1)} %fusion.48), kind=kOutput, calls=%fused_computation.18 | convolution fusion | flops 7548174336 | bytes 16777216 | tf_op jit(solution)/shard_map/dot_general | solution.py:74
  433.6 10.1 %reduce-scatter.2.cloned.1.call-done = bf16[32,3584]{1,0:T(8,128)(2,1)} async-done(((bf16[512,3584]{1,0:T(8,128)(2,1)}), bf16[32,3584]{1,0:T(8,128)(2,1)}) %reduce-scatter.2.cloned.1.call-update) | async-done | bytes 229392 | tf_op jit(solution)/shard_map/reduce_scatter | solution.py:110
  443.6 5.1 %convolution_convert_fusion.5 = bf16[256,3584]{1,0:T(8,128)(2,1)} fusion(bf16[256,3584]{1,0:T(8,128)(2,1)} %bitcast.12, bf16[256,3584]{1,0:T(8,128)(2,1)} %bitcast.6, bf16[32,3584]{1,0:T(8,128)(2,1)} %reduce-scatter.2.cloned.1.call-done, pred[256,256]{1,0:T(32,128)(4,1)S(1)} %get-tuple-element.21, pred[256,256]{1,0:T(32,128)(4,1)S(1)} %get-tuple-element.22, ...), kind=kOutput, calls=%fused_computation.22 | convolution fusion | flops 1011138560 | bytes 5873664 | tf_op jit(solution)/shard_map/dot_general | solution.py:131
  (34 shorter events, 0.1 us)
Async XLA Ops:
  7.2 14.1 %copy-start = (bf16[256,3584]{1,0:T(8,128)(2,1)S(1)}, bf16[256,3584]{1,0:T(8,128)(2,1)}, u32[]{:S(2)}) copy-start(bf16[256,3584]{1,0:T(8,128)(2,1)} %param.5) | copy-start | bytes 5505028
  12.9 47.0 %all-to-all-start.3 = ((bf16[16,16,3584]{2,1,0:T(8,128)(2,1)}), bf16[16,16,3584]{2,1,0:T(8,128)(2,1)}, u32[]{:S(2)}, u32[]{:S(2)}) async-start(bf16[16,16,3584]{2,1,0:T(8,128)(2,1)} %bitcast.61), calls=%async_computation.4 | async-start | bytes 3670016 | tf_op jit(solution)/shard_map/all_to_all | solution.py:26
  59.9 51.9 %all-to-all-start.4 = ((bf16[16,16,3584]{2,1,0:T(8,128)(2,1)}), bf16[16,16,3584]{2,1,0:T(8,128)(2,1)}, u32[]{:S(2)}, u32[]{:S(2)}) async-start(bf16[16,16,3584]{2,1,0:T(8,128)(2,1)} %bitcast.59), calls=%async_computation.5 | async-start | bytes 3670016 | tf_op jit(solution)/shard_map/all_to_all | solution.py:26
  68.8 180.4 %all-gather.5.cloned.1.call-start = ((), (), s32[]{:S(2)}) async-start(), calls=%async_computation.8 | async-start | bytes 3899392 | tf_op jit(solution)/shard_map/all_gather | solution.py:99
  111.8 71.7 %all-to-all-start = ((bf16[16,16,3584]{2,1,0:T(8,128)(2,1)}), bf16[16,16,3584]{2,1,0:T(8,128)(2,1)}, u32[]{:S(2)}, u32[]{:S(2)}) async-start(bf16[16,16,3584]{2,1,0:T(8,128)(2,1)} %bitcast.60), calls=%async_computation.1 | async-start | bytes 3670016 | tf_op jit(solution)/shard_map/all_to_all | solution.py:26
  130.8 61.8 %copy-start.3 = (bf16[256,3584]{1,0:T(8,128)(2,1)S(1)}, bf16[256,3584]{1,0:T(8,128)(2,1)}, u32[]{:S(2)}) copy-start(bf16[256,3584]{1,0:T(8,128)(2,1)} %param.6) | copy-start | bytes 5505028
  183.5 51.6 %all-to-all-start.1 = ((bf16[16,16,3584]{2,1,0:T(8,128)(2,1)}), bf16[16,16,3584]{2,1,0:T(8,128)(2,1)}, u32[]{:S(2)}, u32[]{:S(2)}) async-start(bf16[16,16,3584]{2,1,0:T(8,128)(2,1)} %bitcast.58), calls=%async_computation.2 | async-start | bytes 3670016 | tf_op jit(solution)/shard_map/all_to_all | solution.py:26
  192.3 87.6 %all-gather.3.cloned.1.call-start = ((), (), s32[]{:S(2)}) async-start(), calls=%async_computation.7 | async-start | bytes 3899392 | tf_op jit(solution)/shard_map/all_gather | solution.py:100
  210.5 16.4 %slice-start = ((s8[7340032]{0:T(1024)(128)(4,1)}), s8[4194304]{0:T(1024)(128)(4,1)S(1)}, s32[]{:S(2)}) async-start(s8[7340032]{0:T(1024)(128)(4,1)} %bitcast.62), calls=%async_computation.10 | async-start | bytes 8388608
  216.4 9.9 %copy-start.9 = (bf16[256,1024]{1,0:T(8,128)(2,1)}, bf16[256,1024]{1,0:T(8,128)(2,1)S(1)}, u32[]{:S(2)}) copy-start(bf16[256,1024]{1,0:T(8,128)(2,1)S(1)} %fusion.45) | copy-start | bytes 1572868
  216.4 30.1 %collective-permute-start.4 = (bf16[256,1024]{1,0:T(8,128)(2,1)S(1)}, bf16[256,1024]{1,0:T(8,128)(2,1)}, u32[]{:S(2)}, u32[]{:S(2)}) collective-permute-start(bf16[256,1024]{1,0:T(8,128)(2,1)S(1)} %fusion.45), channel_id=1, source_target_pairs={{0,16},{16,0},{1,17},{17,1},{2,18},{18,2},{3,19},{19,3},{4,20},{20... | collective-permute-start | bytes 1572872 | tf_op jit(solution)/shard_map/ppermute | solution.py:38
  216.5 10.4 %slice-start.1 = ((s8[7340032]{0:T(1024)(128)(4,1)}), s8[3145728]{0:T(1024)(128)(4,1)S(1)}, s32[]{:S(2)}) async-start(s8[7340032]{0:T(1024)(128)(4,1)} %bitcast.62), calls=%async_computation.11 | async-start | bytes 6291456
  226.4 18.5 %collective-permute-start.5 = (bf16[256,2048]{1,0:T(8,128)(2,1)S(1)}, bf16[256,2048]{1,0:T(8,128)(2,1)}, u32[]{:S(2)}, u32[]{:S(2)}) collective-permute-start(bf16[256,2048]{1,0:T(8,128)(2,1)S(1)} %convolution_convert_fusion.13), channel_id=1, source_target_pairs={{0,16},{16,0},{1,17},{17,1},{2,18},{18,2},{3,19},{19,3},{4,20},{20... | collective-permute-start | bytes 3145736 | tf_op jit(solution)/shard_map/ppermute | solution.py:38
  230.5 95.8 %collective-permute-start.2 = (bf16[256,1024]{1,0:T(8,128)(2,1)S(1)}, bf16[256,1024]{1,0:T(8,128)(2,1)}, u32[]{:S(2)}, u32[]{:S(2)}) collective-permute-start(bf16[256,1024]{1,0:T(8,128)(2,1)S(1)} %fusion.42), channel_id=1, source_target_pairs={{0,16},{16,0},{1,17},{17,1},{2,18},{18,2},{3,19},{19,3},{4,20},{20... | collective-permute-start | bytes 1572872 | tf_op jit(solution)/shard_map/ppermute | solution.py:38
  244.8 1.8 copy-start.10
  244.8 80.0 %collective-permute-start.3 = (bf16[256,2048]{1,0:T(8,128)(2,1)S(1)}, bf16[256,2048]{1,0:T(8,128)(2,1)}, u32[]{:S(2)}, u32[]{:S(2)}) collective-permute-start(bf16[256,2048]{1,0:T(8,128)(2,1)S(1)} %convolution_convert_fusion.14), channel_id=1, source_target_pairs={{0,16},{16,0},{1,17},{17,1},{2,18},{18,2},{3,19},{19,3},{4,20},{20... | collective-permute-start | bytes 3145736 | tf_op jit(solution)/shard_map/ppermute | solution.py:38
  262.5 41.1 %collective-permute-start.1 = (bf16[512,2048]{1,0:T(8,128)(2,1)}, bf16[512,2048]{1,0:T(8,128)(2,1)}, u32[]{:S(2)}, u32[]{:S(2)}) collective-permute-start(bf16[512,2048]{1,0:T(8,128)(2,1)} %convolution_convert_fusion.12), channel_id=1, source_target_pairs={{0,16},{16,0},{1,17},{17,1},{2,18},{18,2},{3,19},{19,3},{4,20},{20... | collective-permute-start | bytes 6291464 | tf_op jit(solution)/shard_map/ppermute | solution.py:38
  288.1 11.1 %copy-start.5 = (bf16[512,1024]{1,0:T(8,128)(2,1)}, bf16[512,1024]{1,0:T(8,128)(2,1)S(1)}, u32[]{:S(2)}) copy-start(bf16[512,1024]{1,0:T(8,128)(2,1)S(1)} %fusion.39) | copy-start | bytes 3145732
  288.1 18.7 %collective-permute-start = (bf16[512,1024]{1,0:T(8,128)(2,1)S(1)}, bf16[512,1024]{1,0:T(8,128)(2,1)}, u32[]{:S(2)}, u32[]{:S(2)}) collective-permute-start(bf16[512,1024]{1,0:T(8,128)(2,1)S(1)} %fusion.39), channel_id=1, source_target_pairs={{0,16},{16,0},{1,17},{17,1},{2,18},{18,2},{3,19},{19,3},{4,20},{20... | collective-permute-start | bytes 3145736 | tf_op jit(solution)/shard_map/ppermute | solution.py:38
  299.2 47.9 %all-to-all-start.5 = ((bf16[16,16,3584]{2,1,0:T(8,128)(2,1)}), bf16[16,16,3584]{2,1,0:T(8,128)(2,1)}, u32[]{:S(2)}, u32[]{:S(2)}) async-start(bf16[16,16,3584]{2,1,0:T(8,128)(2,1)} %bitcast.11), calls=%async_computation.6 | async-start | bytes 3670016 | tf_op jit(solution)/shard_map/all_to_all | solution.py:26
  303.6 140.0 %reduce-scatter.2.cloned.1.call-start = ((), (), s32[]{:S(2)}) async-start(), calls=%async_computation.9 | async-start | bytes 3899392 | tf_op jit(solution)/shard_map/reduce_scatter | solution.py:110
  303.6 3.2 copy-start.6
  306.8 3.2 copy-start.2
  310.4 1.3 copy-start.4
  328.1 0.8 copy-start.11
  345.1 15.5 %copy-start.7 = (bf16[256,1024]{1,0:T(8,128)(2,1)S(1)}, bf16[256,1024]{1,0:T(8,128)(2,1)}, u32[]{:S(2)}) copy-start(bf16[256,1024]{1,0:T(8,128)(2,1)} %get-tuple-element.13) | copy-start | bytes 1572868
  345.1 15.5 %copy-start.8 = (bf16[256,1024]{1,0:T(8,128)(2,1)S(1)}, bf16[256,1024]{1,0:T(8,128)(2,1)}, u32[]{:S(2)}) copy-start(bf16[256,1024]{1,0:T(8,128)(2,1)} %get-tuple-element.14) | copy-start | bytes 1572868
  345.1 15.5 %copy-start.12 = (bf16[256,1024]{1,0:T(8,128)(2,1)S(1)}, bf16[256,1024]{1,0:T(8,128)(2,1)}, u32[]{:S(2)}) copy-start(bf16[256,1024]{1,0:T(8,128)(2,1)} %copy-done.11) | copy-start | bytes 1572868
  347.1 86.5 %all-to-all-start.2 = ((bf16[16,16,3584]{2,1,0:T(8,128)(2,1)}), bf16[16,16,3584]{2,1,0:T(8,128)(2,1)}, u32[]{:S(2)}, u32[]{:S(2)}) async-start(bf16[16,16,3584]{2,1,0:T(8,128)(2,1)} %bitcast.5), calls=%async_computation.3 | async-start | bytes 3670016 | tf_op jit(solution)/shard_map/all_to_all | solution.py:26
  418.6 3.3 copy-start.13
  443.6 5.1 %copy-start.1 = (bf16[256,3584]{1,0:T(8,128)(2,1)S(1)}, bf16[256,3584]{1,0:T(8,128)(2,1)}, u32[]{:S(2)}) copy-start(bf16[256,3584]{1,0:T(8,128)(2,1)} %param.5) | copy-start | bytes 5505028
Sparse Core Ops, SparseCore 0:
  72.4 107.2 all-gather.4
  195.9 83.9 all-gather.2
  324.9 118.6 reduce-scatter.1
